TPU v7x, 32 devices: a whole 2x2x4 slice. The times are simulated.
32 devices in a mesh: dp: 2 (over y), expert: 16 (over z, x, core).
Axes of the slice: x: 2, y: 2, z: 4, core: 2. Of those that a mesh axis runs over, the one named last changes fastest.
Arguments:
- inputs_one: bfloat16 [16, 64, 2048], P('expert'), may hold values from -3 to 3
- queries: bfloat16 [16, 64, 2048], P('expert'), may hold values from -14 to 14
- key_heads: bfloat16 [16, 64, 2048], P('expert'), may hold values from -14 to 14
- value_heads: bfloat16 [16, 64, 2048], P('expert'), may hold values from -6 to 6
- groups: int32 [16, 64], P('expert'), may hold values from 0 to 3, never falling along the last dimension, each value on 1 to 32 neighbouring positions
- inputs_two: bfloat16 [16, 64, 2048], P('expert'), may hold values from -3 to 3
- norm_gain: float32 [2048], replicated, may hold values from 0.1 to 1.9
- router: bfloat16 [2048, 64], replicated, may hold values from -0.125 to 0.125
- experts_old: bfloat16 [16, 1024, 3, 4, 2048], P('expert', 'dp'), may hold values from -0.1875 to 0.1875
- routes_one: int32 [16, 64, 8], P('expert'), may hold values from 0 to 63, all different within a row; in each aligned block of 64 rows (0 to 63, 64 to 127, ..., all dimensions but the last counted through in order) at most 16 rows name the same one
- routes_two: int32 [16, 64, 8], P('expert'), may hold values from 0 to 63, all different within a row; in each aligned block of 64 rows (0 to 63, 64 to 127, ..., all dimensions but the last counted through in order) at most 16 rows name the same one
- old_slots: int32 [64], replicated, may hold values from 0 to 63, each once
- new_slots: int32 [80], replicated, may hold values from 0 to 63, as said below
Outputs:
- output_one: bfloat16 [16, 64, 2048], P('expert', 'dp')
- output_two: bfloat16 [16, 64, 2048], P('expert', 'dp')
- experts_new: bfloat16 [16, 1024, 3, 5, 2048], P('expert', 'dp')
Inputs may be any that keep to these rules, and one draw needn't show every extreme that they name: `routes_one`: among the 8 entries of a token no expert repeats, and among the routes of one expert index's 64 tokens no expert is named more than 16 times. `routes_two`: among the 8 entries of a token no expert repeats, and among the routes of one expert index's 64 tokens no expert is named more than 16 times. `groups`: group numbers never fall along a row; each group has 1 to 32 tokens. `old_slots`: each expert fills exactly one slot; slot s of expert index j is entry j * 4 + s. `new_slots`: each expert fills one or two slots, and some fill two; slot s of expert index j is entry j * 5 + s.
All inputs are finite; a program needn't handle non-finite values.
Results may differ from a plain program's by a relative error of at most 0.0062.
Values may be sent and summed in bfloat16 or wider, within the bound.
A program may use at most 192 MiB of HBM per device.

v0:
```python
import jax
import jax.numpy as jnp
from jax import lax
from jax.sharding import PartitionSpec as P

D = 2048
HEADS = 16
HEAD_DIM = 128
EXPERTS = 64
TOPK = 8
MOST = 16


EPS = 1e-06
MASKED = -1e30


def rms_norm(hidden, norm_gain):
    scale = lax.rsqrt(jnp.mean(hidden * hidden, -1, keepdims=True) + EPS)
    return (hidden * scale * norm_gain).astype(jnp.bfloat16)


def pack_rows(normed, flat_slot, slot_total, index_count):
    flat = flat_slot.reshape(-1)
    route_total = flat.shape[0]
    onehot = (flat[:, None] == jnp.arange(slot_total, dtype=jnp.int32)[None, :]).astype(jnp.int32)
    rank = jnp.sum((jnp.cumsum(onehot, 0) - 1) * onehot, 1)
    place = flat * MOST + rank
    source = jnp.full((slot_total * MOST,), route_total, jnp.int32)
    source = source.at[place].set(jnp.arange(route_total, dtype=jnp.int32))
    valid = source < route_total
    token = jnp.minimum(source // TOPK, normed.shape[0] - 1)
    buffer = jnp.where(valid[:, None], normed[token], jnp.zeros((), jnp.bfloat16))
    return (buffer.reshape(index_count, slot_total // index_count, MOST, D), place)


def expert_rows(batch, weights):
    first = jnp.einsum("nsmd,fsd->nsmf", batch, weights[:, 0], preferred_element_type=jnp.float32)
    second = jnp.einsum("nsmd,fsd->nsmf", batch, weights[:, 1], preferred_element_type=jnp.float32)
    act = (jax.nn.silu(first) * second).astype(jnp.bfloat16)
    partial_value = jnp.einsum(
        "nsmf,fsd->nsmd", act, weights[:, 2], preferred_element_type=jnp.float32
    )
    return partial_value.astype(jnp.bfloat16)


def combine_rows(back, place, gates):
    picked = back.reshape(-1, D)[place].astype(jnp.float32)
    picked = picked.reshape(gates.shape[0], TOPK, D)
    return jnp.sum(picked * gates[:, :, None], 1)


def shards(
    inputs_one,
    queries,
    key_heads,
    value_heads,
    groups,
    inputs_two,
    norm_gain,
    router,
    experts_old,
    routes_one,
    routes_two,
    old_slots,
    new_slots,
):
    index_count = lax.axis_size("expert")
    slice_count = lax.axis_size("dp")
    weights_local = experts_old[0]
    hidden_rows = weights_local.shape[0]
    old_width = weights_local.shape[2]
    piece_rows = hidden_rows // index_count
    new_total = new_slots.shape[0]
    new_width = new_total // index_count
    old_total = old_slots.shape[0]
    column = inputs_one.shape[1]
    moving = weights_local.reshape(index_count, piece_rows, 3, old_width, D)
    shape = (column, HEADS, HEAD_DIM)
    scores = jnp.einsum(
        "thd,uhd->htu",
        queries[0].reshape(shape),
        key_heads[0].reshape(shape),
        preferred_element_type=jnp.float32,
    ) * HEAD_DIM ** (-0.5)
    allowed = groups[0][:, None] == groups[0][None, :]
    scores = jnp.where(allowed[None], scores, MASKED)
    row_max = jnp.max(scores, -1, keepdims=True)
    expo = jnp.exp(scores - row_max)
    attn_probs = (expo / jnp.sum(expo, -1, keepdims=True)).astype(jnp.bfloat16)
    context = jnp.einsum(
        "htu,uhd->thd",
        attn_probs,
        value_heads[0].reshape(shape),
        preferred_element_type=jnp.float32,
    ).reshape(column, D)
    hidden_one = inputs_one[0].astype(jnp.float32) + context
    hidden_two = inputs_two[0].astype(jnp.float32)
    normed_one = rms_norm(hidden_one, norm_gain)
    normed_two = rms_norm(hidden_two, norm_gain)
    expert_ids = jnp.arange(EXPERTS, dtype=jnp.int32)
    old_ids = jnp.arange(old_total, dtype=jnp.int32)
    old_place = jnp.sum(
        jnp.where(old_slots[None, :] == expert_ids[:, None], old_ids[None, :], 0), 1
    )
    new_match = new_slots[None, :] == expert_ids[:, None]
    slot_ids = jnp.arange(new_total, dtype=jnp.int32)[None, :]
    first_copy = jnp.min(jnp.where(new_match, slot_ids, new_total), 1)
    last_copy = jnp.max(jnp.where(new_match, slot_ids, -1), 1)

    def route_gates(normed, chosen_hot):
        logits = jnp.dot(normed, router, preferred_element_type=jnp.float32)
        chosen = jnp.sum(jnp.where(chosen_hot, logits[:, None, :], 0.0), -1)
        sig = jax.nn.sigmoid(chosen)
        return sig / jnp.sum(sig, -1, keepdims=True)

    hot_one = routes_one[0][:, :, None] == expert_ids[None, None, :]
    hot_two = routes_two[0][:, :, None] == expert_ids[None, None, :]
    gates_one = route_gates(normed_one, hot_one)
    gates_two = route_gates(normed_two, hot_two)
    slot_one = jnp.sum(jnp.where(hot_one, old_place[None, None, :], 0), -1)
    parity = (
        jnp.arange(column, dtype=jnp.int32)[:, None] + jnp.arange(TOPK, dtype=jnp.int32)[None, :]
    ) % 2
    first_pick = jnp.sum(jnp.where(hot_two, first_copy[None, None, :], 0), -1)
    last_pick = jnp.sum(jnp.where(hot_two, last_copy[None, None, :], 0), -1)
    slot_two = jnp.where(parity == 0, first_pick, last_pick)
    buffer_one, place_one = pack_rows(normed_one, slot_one, old_total, index_count)
    buffer_two, place_two = pack_rows(normed_two, slot_two, new_total, index_count)
    sent_one, sent_two, spread = (
        lax.all_to_all(buffer_one, "expert", split_axis=0, concat_axis=0, tiled=True),
        lax.all_to_all(buffer_two, "expert", split_axis=0, concat_axis=0, tiled=True),
        lax.all_to_all(moving, "expert", split_axis=0, concat_axis=0, tiled=True),
    )
    part_one = expert_rows(sent_one, weights_local)
    table = jnp.moveaxis(spread, 3, 1).reshape(index_count * old_width, piece_rows, 3, D)
    new_place = jnp.sum(
        jnp.where(new_slots[:, None] == expert_ids[None, :], old_place[None, :], 0), 1
    )
    outgoing = table[new_place].reshape(index_count, new_width, piece_rows, 3, D)
    arrived = lax.all_to_all(outgoing, "expert", split_axis=0, concat_axis=0, tiled=True)
    weights_new = jnp.transpose(arrived, (0, 2, 3, 1, 4)).reshape(hidden_rows, 3, new_width, D)
    part_two = expert_rows(sent_two, weights_new)
    back_one, back_two = (
        lax.all_to_all(part_one, "expert", split_axis=0, concat_axis=0, tiled=True),
        lax.all_to_all(part_two, "expert", split_axis=0, concat_axis=0, tiled=True),
    )
    mixed_one = combine_rows(back_one, place_one, gates_one)
    mixed_two = combine_rows(back_two, place_two, gates_two)
    summed_one, summed_two = (
        lax.psum_scatter(mixed_one, "dp", scatter_dimension=0, tiled=True),
        lax.psum_scatter(mixed_two, "dp", scatter_dimension=0, tiled=True),
    )
    own_rows = column // slice_count
    start = lax.axis_index("dp") * own_rows
    own_one = lax.dynamic_slice_in_dim(hidden_one, start, own_rows, 0)
    own_two = lax.dynamic_slice_in_dim(hidden_two, start, own_rows, 0)
    output_one = (own_one + summed_one).astype(jnp.bfloat16)[None]
    output_two = (own_two + summed_two).astype(jnp.bfloat16)[None]
    return (output_one, output_two, weights_new[None])


def solution(mesh):
    in_specs = (
        P("expert", None, None),
        P("expert", None, None),
        P("expert", None, None),
        P("expert", None, None),
        P("expert", None),
        P("expert", None, None),
        P(),
        P(),
        P("expert", "dp", None, None, None),
        P("expert", None, None),
        P("expert", None, None),
        P(),
        P(),
    )
    out_specs = (
        P("expert", "dp", None),
        P("expert", "dp", None),
        P("expert", "dp", None, None, None),
    )
    return jax.shard_map(shards, mesh=mesh, in_specs=in_specs, out_specs=out_specs, check_vma=False)
```

profile of v0, /device:TPU:15, one launch (start us, length us, event | category | flops | bytes accessed | tf_op | source)
XLA Modules:
  0.0 1728.5 jit_solution(4144757228547257335)
XLA Ops:
  7.2 0.8 select_reduce_fusion.8
  8.0 0.8 copy.111
  8.8 1.2 select_reduce_fusion.4
  10.4 1.2 reduce-window.14
  12.0 2.4 scatter_custom_fusion
  14.5 1.1 fusion.32
  15.6 1.0 convert_bitcast_fusion.2
  16.7 1.0 copy.146
  17.7 1.0 copy.145
  19.9 1.0 multiply_convert_fusion
  20.9 6.0 gather_fusion
  26.9 4.5 broadcast_select_fusion.1
  31.3 6.6 all-to-all-start
  37.9 26.8 %copy.121 = bf16[16,32,3,4,2048]{4,1,3,2,0:T(8,128)(2,1)} copy(bf16[16,32,3,4,2048]{4,3,2,1,0:T(4,128)(2,1)} %bitcast.208) | data formatting | bytes 50331648 | tf_op jit(solution)/shard_map/reshape;squeeze | solution.py:78
  64.7 65.6 %all-to-all-done = bf16[16,4,16,2048]{3,2,1,0:T(8,128)(2,1)} async-done(((bf16[16,4,16,2048]{3,2,1,0:T(8,128)(2,1)}), bf16[16,4,16,2048]{3,2,1,0:T(8,128)(2,1)}, u32[]{:S(2)}, u32[]{:S(2)}) %all-to-all-start) | async-done | bytes 4194336 | tf_op jit(solution)/shard_map/all_to_all | solution.py:131
  130.3 5.4 all-to-all-start.2
  136.0 2.3 select_reduce_fusion.1
  139.2 1.2 reduce-window.16
  140.9 2.6 scatter_custom_fusion.1
  143.7 6.3 gather_fusion.3
  150.0 5.3 broadcast_select_fusion
  155.3 522.0 %all-to-all-done.2 = bf16[16,32,3,4,2048]{4,1,3,2,0:T(8,128)(2,1)} async-done(((bf16[16,32,3,4,2048]{4,1,3,2,0:T(8,128)(2,1)}), bf16[16,32,3,4,2048]{4,1,3,2,0:T(8,128)(2,1)}, u32[]{:S(2)}, u32[]{:S(2)}) %all-to-all-start.2) | async-done | bytes 25165856 | tf_op jit(solution)/shard_map/all_to_all | solution.py:133
  677.2 4.8 all-to-all-start.4
  682.2 21.0 %copy.122 = bf16[16,32,3,4,2048]{4,1,2,3,0:T(8,128)(2,1)} copy(bf16[16,32,3,4,2048]{4,1,3,2,0:T(8,128)(2,1)} %all-to-all-done.2) | data formatting | bytes 50331648 | tf_op jit(solution)/shard_map/all_to_all | solution.py:133
  703.2 20.8 %gather_fusion.2 = bf16[80,32,3,2048]{3,1,2,0:T(8,128)(2,1)} fusion(bf16[64,32,3,2048]{3,1,2,0:T(8,128)(2,1)} %bitcast.206, s32[1024]{0:T(1024)S(1)} %pad_clamp_fusion.2), kind=kCustom, calls=%fused_computation.2 | custom fusion | bytes 62914880 | tf_op jit(solution)/shard_map/gather | solution.py:140
  724.0 73.0 %all-to-all-done.4 = bf16[16,5,16,2048]{3,2,1,0:T(8,128)(2,1)} async-done(((bf16[16,5,16,2048]{3,2,1,0:T(8,128)(2,1)}), bf16[16,5,16,2048]{3,2,1,0:T(8,128)(2,1)}, u32[]{:S(2)}, u32[]{:S(2)}) %all-to-all-start.4) | async-done | bytes 5242912 | tf_op jit(solution)/shard_map/all_to_all | solution.py:132
  797.0 5.7 all-to-all-start.3
  802.7 26.8 %copy.176 = bf16[1,512,3,4,2048]{4,1,3,2,0:T(8,128)(2,1)} copy(bf16[1,512,3,4,2048]{4,3,2,1,0:T(4,128)(2,1)} %param.21) | data formatting | bytes 50331648 | tf_op args[8]
  829.5 7.0 fusion.6
  836.5 10.9 convert_bitcast_fusion.1
  847.5 4.7 copy.117
  852.2 626.8 %all-to-all-done.3 = bf16[16,5,32,3,2048]{4,2,3,1,0:T(8,128)(2,1)} async-done(((bf16[16,5,32,3,2048]{4,2,3,1,0:T(8,128)(2,1)}), bf16[16,5,32,3,2048]{4,2,3,1,0:T(8,128)(2,1)}, u32[]{:S(2)}, u32[]{:S(2)}) %all-to-all-start.3) | async-done | bytes 31457312 | tf_op jit(solution)/shard_map/all_to_all | solution.py:141
  1479.0 5.0 all-to-all-start.1
  1484.0 21.3 %copy.123 = bf16[16,32,3,5,2048]{4,1,0,3,2:T(8,128)(2,1)} copy(bf16[16,32,3,5,2048]{4,1,2,3,0:T(8,128)(2,1)} %bitcast.31) | data formatting | bytes 62914560 | tf_op jit(solution)/shard_map/transpose | solution.py:142
  1505.3 7.2 fusion.2
  1512.6 8.5 fusion.13
  1521.1 9.5 convert_bitcast_fusion
  1530.6 5.7 copy.128
  1536.3 40.1 %all-to-all-done.1 = bf16[16,4,16,2048]{3,2,1,0:T(8,128)(2,1)} async-done(((bf16[16,4,16,2048]{3,2,1,0:T(8,128)(2,1)}), bf16[16,4,16,2048]{3,2,1,0:T(8,128)(2,1)}, u32[]{:S(2)}, u32[]{:S(2)}) %all-to-all-start.1) | async-done | bytes 4194336 | tf_op jit(solution)/shard_map/all_to_all | solution.py:145
  1576.3 4.9 all-to-all-start.5
  1582.0 7.2 gather_fusion.1
  1589.2 2.6 fusion.10
  1592.8 103.3 %all-to-all-done.5 = bf16[16,5,16,2048]{3,2,1,0:T(8,128)(2,1)} async-done(((bf16[16,5,16,2048]{3,2,1,0:T(8,128)(2,1)}), bf16[16,5,16,2048]{3,2,1,0:T(8,128)(2,1)}, u32[]{:S(2)}, u32[]{:S(2)}) %all-to-all-start.5) | async-done | bytes 5242912 | tf_op jit(solution)/shard_map/all_to_all | solution.py:146
  1696.1 7.6 gather_fusion.4
  1703.8 2.6 fusion.9
  1706.5 1.6 fusion.46
  1708.2 11.5 reduce-scatter.5.cloned.1.call-done
  1719.6 1.6 fusion.47
  (113 shorter events, 5.4 us)
Async XLA Ops:
  7.2 1574.1 %copy-start = (bf16[2048,64]{0,1:T(8,128)(2,1)S(1)}, bf16[2048,64]{0,1:T(8,128)(2,1)}, u32[]{:S(2)}) copy-start(bf16[2048,64]{0,1:T(8,128)(2,1)} %param.20) | copy-start | bytes 786436
  7.2 11.6 copy-start.13
  7.2 11.6 copy-start.20
  8.8 1.5 copy-start.11
  12.0 4.8 copy-start.15
  12.0 7.9 copy-start.5
  12.0 7.9 copy-start.8
  12.0 7.9 copy-start.14
  20.9 6.0 copy-start.3
  20.9 122.8 %copy-start.1 = (bf16[64,2048]{1,0:T(8,128)(2,1)}, bf16[64,2048]{1,0:T(8,128)(2,1)S(1)}, u32[]{:S(2)}) copy-start(bf16[64,2048]{1,0:T(8,128)(2,1)S(1)} %get-tuple-element.9) | copy-start | bytes 786436
  31.3 99.0 %all-to-all-start = ((bf16[16,4,16,2048]{3,2,1,0:T(8,128)(2,1)}), bf16[16,4,16,2048]{3,2,1,0:T(8,128)(2,1)}, u32[]{:S(2)}, u32[]{:S(2)}) async-start(bf16[16,4,16,2048]{3,2,1,0:T(8,128)(2,1)} %broadcast_select_fusion.1), calls=%async_computation | async-start | bytes 8388608 | tf_op jit(solution)/shard_map/all_to_all | solution.py:131
  64.7 71.0 %copy-start.19 = (s32[1,64,8]{1,2,0:T(8,128)S(1)}, s32[1,64,8]{1,2,0:T(8,128)}, u32[]{:S(2)}) copy-start(s32[1,64,8]{1,2,0:T(8,128)} %param.23) | copy-start | bytes 6148
  64.7 71.1 %copy-start.21 = (s32[80]{0:T(128)S(1)}, s32[80]{0:T(128)}, u32[]{:S(2)}) copy-start(s32[80]{0:T(128)} %param.25) | copy-start | bytes 964
  130.3 546.9 %all-to-all-start.2 = ((bf16[16,32,3,4,2048]{4,1,3,2,0:T(8,128)(2,1)}), bf16[16,32,3,4,2048]{4,1,3,2,0:T(8,128)(2,1)}, u32[]{:S(2)}, u32[]{:S(2)}) async-start(bf16[16,32,3,4,2048]{4,1,3,2,0:T(8,128)(2,1)} %copy.121), calls=%async_computation.3 | async-start | bytes 50331648 | tf_op jit(solution)/shard_map/all_to_all | solution.py:133
  135.9 2.7 copy-start.9
  140.9 2.7 copy-start.17
  677.2 119.8 %all-to-all-start.4 = ((bf16[16,5,16,2048]{3,2,1,0:T(8,128)(2,1)}), bf16[16,5,16,2048]{3,2,1,0:T(8,128)(2,1)}, u32[]{:S(2)}, u32[]{:S(2)}) async-start(bf16[16,5,16,2048]{3,2,1,0:T(8,128)(2,1)} %broadcast_select_fusion), calls=%async_computation.5 | async-start | bytes 10485760 | tf_op jit(solution)/shard_map/all_to_all | solution.py:132
  797.0 682.0 %all-to-all-start.3 = ((bf16[16,5,32,3,2048]{4,2,3,1,0:T(8,128)(2,1)}), bf16[16,5,32,3,2048]{4,2,3,1,0:T(8,128)(2,1)}, u32[]{:S(2)}, u32[]{:S(2)}) async-start(bf16[16,5,32,3,2048]{4,2,3,1,0:T(8,128)(2,1)} %bitcast.207), calls=%async_computation.4 | async-start | bytes 62914560 | tf_op jit(solution)/shard_map/all_to_all | solution.py:141
  1479.0 97.3 %all-to-all-start.1 = ((bf16[16,4,16,2048]{3,2,1,0:T(8,128)(2,1)}), bf16[16,4,16,2048]{3,2,1,0:T(8,128)(2,1)}, u32[]{:S(2)}, u32[]{:S(2)}) async-start(bf16[16,4,16,2048]{3,2,1,0:T(8,128)(2,1)} %copy.117), calls=%async_computation.1 | async-start | bytes 8388608 | tf_op jit(solution)/shard_map/all_to_all | solution.py:145
  1536.3 45.0 %copy-start.4 = (bf16[64,2048]{1,0:T(8,128)(2,1)S(1)}, bf16[64,2048]{1,0:T(8,128)(2,1)}, u32[]{:S(2)}) copy-start(bf16[64,2048]{1,0:T(8,128)(2,1)} %copy-done.3) | copy-start | bytes 786436
  1536.3 45.2 %copy-start.12 = (s32[64,8]{1,0:T(8,128)S(1)}, s32[64,8]{1,0:T(8,128)}, u32[]{:S(2)}) copy-start(s32[64,8]{1,0:T(8,128)} %copy-done.11) | copy-start | bytes 6148
  1536.3 45.7 %copy-start.16 = (s32[512,1]{0,1:T(1,128)S(1)}, s32[512,1]{0,1:T(1,128)}, u32[]{:S(2)}) copy-start(s32[512,1]{0,1:T(1,128)} %copy-done.15) | copy-start | bytes 6148
  1576.3 119.8 %all-to-all-start.5 = ((bf16[16,5,16,2048]{3,2,1,0:T(8,128)(2,1)}), bf16[16,5,16,2048]{3,2,1,0:T(8,128)(2,1)}, u32[]{:S(2)}, u32[]{:S(2)}) async-start(bf16[16,5,16,2048]{3,2,1,0:T(8,128)(2,1)} %copy.128), calls=%async_computation.6 | async-start | bytes 10485760 | tf_op jit(solution)/shard_map/all_to_all | solution.py:146
  1581.2 125.3 %reduce-scatter.3.cloned.1.call-start = ((), (), s32[]{:S(2)}) async-start(), calls=%async_computation.8 | async-start | bytes 786432 | tf_op jit(solution)/shard_map/reduce_scatter | solution.py:151
  1582.0 10.2 copy-start.2
  1582.0 10.4 copy-start.10
  1582.0 10.8 copy-start.18
  1591.8 127.8 %reduce-scatter.5.cloned.1.call-start = ((), (), s32[]{:S(2)}) async-start(), calls=%async_computation.9 | async-start | bytes 786432 | tf_op jit(solution)/shard_map/reduce_scatter | solution.py:152
  1696.1 10.3 copy-start.6
  1696.1 10.4 copy-start.7
Sparse Core Ops, SparseCore 0:
  1591.9 14.1 reduce-scatter.2
  1706.5 13.0 reduce-scatter.4
where the time goes:
time: 1740 us; the launch traced here: 1730 us
  waiting for transfers between devices  1440 us (83%)
  local copies, waits for them, and re-layouts  164 us (9%)
  matrix products  44.4 us (3%)
  starting transfers between devices  32.7 us (2%)
  other arithmetic  29.6 us (2%)
    all_to_all x1, waiting for transfers between devices, shards(): lax.all_to_all(outgoing, 'expert', split_axis=0, concat_axis=0, tiled=True)  627 us
    all_to_all x1, waiting for transfers between devices, shards(): lax.all_to_all(moving, 'expert', split_axis=0, concat_axis=0, tiled=True)  522 us
    all_to_all x1, waiting for transfers between devices, shards(): lax.all_to_all(part_two, 'expert', split_axis=0, concat_axis=0, tiled=True)  103 us
    all_to_all x1, waiting for transfers between devices, shards(): lax.all_to_all(buffer_two, 'expert', split_axis=0, concat_axis=0, tiled=T...  73 us
    all_to_all x1, waiting for transfers between devices, shards(): lax.all_to_all(buffer_one, 'expert', split_axis=0, concat_axis=0, tiled=T...  65.6 us
    all_to_all x1, waiting for transfers between devices, shards(): lax.all_to_all(part_one, 'expert', split_axis=0, concat_axis=0, tiled=True)  40.1 us
  transfers between devices with their start and end apart: 8, of which 7 were waited for; matrix products, arithmetic and copies ran while one was open for 12% of the time, Pallas kernels for 0%

commit v1 on v0

v1 whole, which is shorter than its diff:
```python
import jax
import jax.numpy as jnp
from jax import lax
from jax.sharding import PartitionSpec as P

D = 2048
HEADS = 16
HEAD_DIM = 128
EXPERTS = 64


EPS = 1e-06
MASKED = -1e30


def rms_norm(hidden, norm_gain):
    scale = lax.rsqrt(jnp.mean(hidden * hidden, -1, keepdims=True) + EPS)
    return (hidden * scale * norm_gain).astype(jnp.bfloat16)


def shards(
    inputs_one,
    queries,
    key_heads,
    value_heads,
    groups,
    inputs_two,
    norm_gain,
    router,
    experts_old,
    routes_one,
    routes_two,
    old_slots,
    new_slots,
):
    index_count = lax.axis_size("expert")
    slice_count = lax.axis_size("dp")
    weights_local = experts_old[0]
    hidden_rows = weights_local.shape[0]
    old_width = weights_local.shape[2]
    piece_rows = hidden_rows // index_count
    new_total = new_slots.shape[0]
    new_width = new_total // index_count
    old_total = old_slots.shape[0]
    column = inputs_one.shape[1]
    own_rows = column // slice_count
    moving = jnp.transpose(
        weights_local.reshape(index_count, piece_rows, 3, old_width, D), (0, 2, 3, 1, 4)
    )
    spread = lax.all_to_all(moving, "expert", split_axis=0, concat_axis=0, tiled=True)
    shape = (column, HEADS, HEAD_DIM)
    scores = jnp.einsum(
        "thd,uhd->htu",
        queries[0].reshape(shape),
        key_heads[0].reshape(shape),
        preferred_element_type=jnp.float32,
    ) * HEAD_DIM ** (-0.5)
    allowed = groups[0][:, None] == groups[0][None, :]
    scores = jnp.where(allowed[None], scores, MASKED)
    row_max = jnp.max(scores, -1, keepdims=True)
    expo = jnp.exp(scores - row_max)
    attn_probs = (expo / jnp.sum(expo, -1, keepdims=True)).astype(jnp.bfloat16)
    context = jnp.einsum(
        "htu,uhd->thd",
        attn_probs,
        value_heads[0].reshape(shape),
        preferred_element_type=jnp.float32,
    ).reshape(column, D)
    hidden_one = inputs_one[0].astype(jnp.float32) + context
    hidden_two = inputs_two[0].astype(jnp.float32)
    normed_one = rms_norm(hidden_one, norm_gain)
    normed_two = rms_norm(hidden_two, norm_gain)
    expert_ids = jnp.arange(EXPERTS, dtype=jnp.int32)
    old_ids = jnp.arange(old_total, dtype=jnp.int32)
    old_place = jnp.sum(
        jnp.where(old_slots[None, :] == expert_ids[:, None], old_ids[None, :], 0), 1
    )

    def slot_gates(normed, routes):
        logits = jnp.dot(normed, router, preferred_element_type=jnp.float32)
        chosen_hot = routes[:, :, None] == expert_ids[None, None, :]
        picked = jnp.where(jnp.any(chosen_hot, 1), jax.nn.sigmoid(logits), 0.0)
        gates = picked / jnp.sum(picked, -1, keepdims=True)
        slot_hot = (old_slots[None, :] == expert_ids[:, None]).astype(jnp.float32)
        return jnp.dot(gates, slot_hot, precision=lax.Precision.HIGHEST)

    def side_by_side(one, two):
        split = (slice_count, 1, own_rows, one.shape[-1])
        return jnp.concatenate([one.reshape(split), two.reshape(split)], 1).reshape(
            2 * column, one.shape[-1]
        )

    gates = side_by_side(
        slot_gates(normed_one, routes_one[0]), slot_gates(normed_two, routes_two[0])
    )
    tokens = lax.all_gather(side_by_side(normed_one, normed_two), "expert", tiled=True)
    own_gates = lax.all_to_all(
        jnp.moveaxis(gates.reshape(2 * column, index_count, old_width), 1, 0),
        "expert",
        split_axis=0,
        concat_axis=0,
        tiled=True,
    ).reshape(index_count * 2 * column, old_width)
    first = jnp.einsum("td,nsfd->tnsf", tokens, moving[:, 0], preferred_element_type=jnp.float32)
    second = jnp.einsum("td,nsfd->tnsf", tokens, moving[:, 1], preferred_element_type=jnp.float32)
    act = (jax.nn.silu(first) * second * own_gates[:, None, :, None]).astype(jnp.bfloat16)
    mixed = jnp.einsum("tnsf,nsfd->td", act, moving[:, 2], preferred_element_type=jnp.float32)
    spread, mixed = lax.optimization_barrier((spread, mixed))
    summed = lax.psum_scatter(mixed, ("expert", "dp"), scatter_dimension=0, tiled=True)
    summed = summed.reshape(2, own_rows, D)
    start = lax.axis_index("dp") * own_rows
    own_one = lax.dynamic_slice_in_dim(hidden_one, start, own_rows, 0)
    own_two = lax.dynamic_slice_in_dim(hidden_two, start, own_rows, 0)
    output_one = (own_one + summed[0]).astype(jnp.bfloat16)[None]
    output_two = (own_two + summed[1]).astype(jnp.bfloat16)[None]

    table = jnp.moveaxis(spread, 2, 1).reshape(index_count * old_width, 3, piece_rows, D)
    new_place = jnp.sum(
        jnp.where(new_slots[:, None] == expert_ids[None, :], old_place[None, :], 0), 1
    )
    outgoing = table[new_place].reshape(index_count, new_width, 3, piece_rows, D)
    arrived = lax.all_to_all(outgoing, "expert", split_axis=0, concat_axis=0, tiled=True)
    weights_new = jnp.transpose(arrived, (0, 3, 2, 1, 4)).reshape(hidden_rows, 3, new_width, D)
    return (output_one, output_two, weights_new[None])


def solution(mesh):
    in_specs = (
        P("expert", None, None),
        P("expert", None, None),
        P("expert", None, None),
        P("expert", None, None),
        P("expert", None),
        P("expert", None, None),
        P(),
        P(),
        P("expert", "dp", None, None, None),
        P("expert", None, None),
        P("expert", None, None),
        P(),
        P(),
    )
    out_specs = (
        P("expert", "dp", None),
        P("expert", "dp", None),
        P("expert", "dp", None, None, None),
    )
    return jax.shard_map(shards, mesh=mesh, in_specs=in_specs, out_specs=out_specs, check_vma=False)
```

time: 1740 us -> 1500 us (0.86)
  waiting for transfers between devices: 1440 us -> 1240 us
  matrix products: 44.4 us -> 78.8 us
  other arithmetic: 29.6 us -> 9.62 us
  local copies, waits for them, and re-layouts: 164 us -> 146 us
    reduce_scatter x2 -> x1, waiting for transfers between devices: 11.5 us -> 746 us  [shards(): lax.psum_scatter(mixed, ('expert', 'dp'), scatter_dimension=0, tiled=True)]
    all_to_all x1, waiting for transfers between devices: 627 us -> 28 us  [shards(): lax.all_to_all(outgoing, 'expert', split_axis=0, concat_axis=0, tiled=True)]
    all_to_all x4 -> x1, waiting for transfers between devices: 282 us -> 0.01 us  [shards(): lax.all_to_all(jnp.moveaxis(gates.reshape(2 * column, index_count, old_wi...]
    all_to_all x1, waiting for transfers between devices: 522 us -> 419 us  [shards(): lax.all_to_all(moving, 'expert', split_axis=0, concat_axis=0, tiled=True)]
    all_gather x0 -> x1, waiting for transfers between devices: none -> 43 us  [shards(): lax.all_gather(side_by_side(normed_one, normed_two), 'expert', tiled=True)]
    dot_general x7, matrix products: 43.7 us -> 78 us  [the longest x1 28.5 us: shards(): jnp.einsum('td,nsfd->tnsf', tokens, moving[:, 0], preferred_element_type=...]
    gather x5 -> x1, local copies, waits for them, and re-layouts: 47.9 us -> 21 us  [shards(): table[new_place].reshape(index_count, new_width, 3, piece_rows, D)]
    unnamed x49 -> x26, local copies, waits for them, and re-layouts: 29 us -> 3.92 us
  transfers between devices with their start and end apart: 8 -> 5, of which waited for: 7 -> 4; matrix products, arithmetic and copies ran while one was open for 12% -> 9% of each run, Pallas kernels for 0% -> 0%
where the time goes in v1:
time: 1500 us
  waiting for transfers between devices  1240 us (83%)
  local copies, waits for them, and re-layouts  146 us (10%)
  matrix products  78.8 us (5%)
  starting transfers between devices  18.3 us (1%)
    reduce_scatter x1, waiting for transfers between devices, shards(): lax.psum_scatter(mixed, ('expert', 'dp'), scatter_dimension=0, tiled=True)  746 us
    all_to_all x1, waiting for transfers between devices, shards(): lax.all_to_all(moving, 'expert', split_axis=0, concat_axis=0, tiled=True)  419 us
    all_gather x1, waiting for transfers between devices, shards(): lax.all_gather(side_by_side(normed_one, normed_two), 'expert', tiled=True)  43 us
  transfers between devices with their start and end apart: 5, of which 4 were waited for; matrix products, arithmetic and copies ran while one was open for 9% of the time, Pallas kernels for 0%

profile of v1, /device:TPU:15, one launch (start us, length us, event | category | flops | bytes accessed | tf_op | source)
XLA Modules:
  0.0 1502.7 jit_solution(16900584378825162860)
XLA Ops:
  7.3 1.1 convert_element_type.101
  8.4 1.3 fusion.20
  9.6 1.0 copy.100
  10.7 1.0 copy.101
  11.6 0.8 broadcast_compare_fusion
  12.5 0.3 fusion.11
  12.7 0.1 fusion.53
  12.9 1.0 convert_bitcast_fusion
  13.9 0.1 copy.103
  14.0 1.0 copy.102
  15.0 0.5 fusion.24
  15.5 0.3 copy.77
  16.1 1.1 multiply_convert_fusion.3
  17.3 0.9 copy.83
  18.1 0.8 copy.84
  18.9 0.2 fusion.38
  19.2 1.0 bitcast_add_fusion
  20.2 0.8 copy-done.2
  21.0 0.3 fusion.55
  21.4 0.2 fusion.44
  21.6 0.1 copy.88
  21.8 0.2 fusion.39
  22.1 0.3 fusion.54
  22.4 0.2 fusion.42
  22.6 0.1 copy.89
  22.7 0.2 pad_maximum_fusion.1
  22.9 0.8 reshape_reshape.3
  23.6 6.6 all-to-all-start.1
  30.2 26.8 %copy.120 = bf16[16,32,3,4,2048]{4,1,3,2,0:T(8,128)(2,1)} copy(bf16[16,32,3,4,2048]{4,3,2,1,0:T(4,128)(2,1)} %bitcast.115) | data formatting | bytes 50331648 | tf_op jit(solution)/shard_map/transpose | solution.py:47
  57.0 6.0 all-to-all-start
  63.1 26.8 %copy.121 = bf16[16,32,3,4,2048]{4,1,3,0,2:T(8,128)(2,1)} copy(bf16[16,32,3,4,2048]{4,3,2,1,0:T(4,128)(2,1)} %bitcast.116) | data formatting | bytes 50331648 | tf_op jit(solution)/shard_map/reshape;squeeze | solution.py:48
  89.9 0.1 select_reduce_fusion.1
  90.0 0.1 select_reduce_fusion
  90.1 0.6 pad_clamp_fusion
  90.7 43.0 %all-gather.2.cloned.1.call-done = bf16[2048,2048]{1,0:T(8,128)(2,1)} async-done(((bf16[128,2048]{1,0:T(8,128)(2,1)}), bf16[2048,2048]{1,0:T(8,128)(2,1)}) %all-gather.2.cloned.1.call-update) | async-done | bytes 8388624 | tf_op jit(solution)/shard_map/all_gather | solution.py:96
  133.8 24.1 %fusion.3 = f32[2048,16,4,32]{0,3,2,1:T(8,128)} fusion(bf16[16,3,4,32,2048]{4,3,2,0,1:T(8,128)(2,1)} %bitcast.119, bf16[2048,2048]{1,0:T(8,128)(2,1)} %all-gather.2.cloned.1.call-done), kind=kOutput, calls=%fused_computation.9 | convolution fusion | flops 17179869184 | bytes 33554432 | tf_op jit(solution)/shard_map/td,nsfd->tnsf/dot_general | solution.py:105
  157.9 28.5 %multiply_convert_fusion.clone.7 = bf16[2048,16,4,32]{0,3,2,1:T(8,128)(2,1)} fusion(f32[2048,16,4,32]{0,3,2,1:T(8,128)} %fusion.3, bf16[16,3,4,32,2048]{4,3,2,0,1:T(8,128)(2,1)} %bitcast.120, bf16[2048,2048]{1,0:T(8,128)(2,1)} %all-gather.2.cloned.1.call-done, f32[2048,4]{0,1:T(4,128)S(1)} %bitcast.135), kind=kOutput, calls=%fused_computation.4.clone.clone.clone.clone.clone.2 | convolution fusion | flops 17209229312 | bytes 41975808 | tf_op jit(solution)/shard_map/td,nsfd->tnsf/dot_general | solution.py:104
  186.4 24.3 %fusion.2 = f32[2048,2048]{1,0:T(8,128)} fusion(bf16[16,3,4,32,2048]{4,3,2,0,1:T(8,128)(2,1)} %bitcast.121, bf16[2048,16,4,32]{0,3,2,1:T(8,128)(2,1)} %multiply_convert_fusion.clone.7), kind=kOutput, calls=%fused_computation.6 | convolution fusion | flops 17179869184 | bytes 33554432 | tf_op jit(solution)/shard_map/tnsf,nsfd->td/dot_general | solution.py:107
  210.7 418.6 %all-to-all-done = bf16[16,3,4,32,2048]{4,3,2,1,0:T(8,128)(2,1)} async-done(((bf16[16,3,4,32,2048]{4,3,2,1,0:T(8,128)(2,1)}), bf16[16,3,4,32,2048]{4,3,2,1,0:T(8,128)(2,1)}, u32[]{:S(2)}, u32[]{:S(2)}) %all-to-all-start) | async-done | bytes 25165856 | tf_op jit(solution)/shard_map/all_to_all | solution.py:50
  629.3 21.0 %copy.90 = bf16[16,3,4,32,2048]{4,3,1,2,0:T(8,128)(2,1)} copy(bf16[16,3,4,32,2048]{4,3,2,1,0:T(8,128)(2,1)} %all-to-all-done) | data formatting | bytes 50331648 | tf_op jit(solution)/shard_map/optimization_barrier | solution.py:108
  650.3 21.0 %gather_fusion = bf16[80,3,32,2048]{3,2,1,0:T(8,128)(2,1)} fusion(bf16[64,3,32,2048]{3,2,1,0:T(8,128)(2,1)} %bitcast.113, s32[1024]{0:T(1024)} %pad_clamp_fusion), kind=kCustom, calls=%fused_computation | custom fusion | bytes 62914880 | tf_op jit(solution)/shard_map/gather | solution.py:121
  671.3 21.4 %copy.91 = bf16[16,5,3,32,2048]{4,3,1,2,0:T(8,128)(2,1)} copy(bf16[16,5,3,32,2048]{4,3,2,1,0:T(8,128)(2,1)} %bitcast.114) | data formatting | bytes 62914560 | tf_op jit(solution)/shard_map/reshape | solution.py:121
  692.7 5.7 all-to-all-start.2
  698.4 0.7 reduce-scatter.2.cloned.1.call-update
  699.1 745.6 %reduce-scatter.2.cloned.1.call-done = f32[64,2048]{1,0:T(8,128)} async-done(((f32[2048,2048]{1,0:T(8,128)}), f32[64,2048]{1,0:T(8,128)}) %reduce-scatter.2.cloned.1.call-update) | async-done | bytes 524304 | tf_op jit(solution)/shard_map/reduce_scatter | solution.py:109
  1444.7 1.8 fusion.41
  1446.6 28.0 %all-to-all-done.2 = bf16[16,5,3,32,2048]{4,3,1,2,0:T(8,128)(2,1)} async-done(((bf16[16,5,3,32,2048]{4,3,1,2,0:T(8,128)(2,1)}), bf16[16,5,3,32,2048]{4,3,1,2,0:T(8,128)(2,1)}, u32[]{:S(2)}, u32[]{:S(2)}) %all-to-all-start.2) | async-done | bytes 31457312 | tf_op jit(solution)/shard_map/all_to_all | solution.py:122
  1474.6 21.3 %copy.92 = bf16[16,5,3,32,2048]{4,3,0,1,2:T(8,128)(2,1)} copy(bf16[16,5,3,32,2048]{4,3,1,2,0:T(8,128)(2,1)} %all-to-all-done.2) | data formatting | bytes 62914560 | tf_op jit(solution)/shard_map/all_to_all | solution.py:122
  (35 shorter events, 0.7 us)
Async XLA Ops:
  7.2 13.8 copy-start
  7.2 14.9 copy-start.6
  7.2 13.8 copy-start.7
  7.2 14.1 copy-start.9
  7.2 14.5 copy-start.8
  7.2 126.5 %all-gather.2.cloned.1.call-start = ((), (), s32[]{:S(2)}) async-start(), calls=%async_computation.4 | async-start | bytes 8912896 | tf_op jit(solution)/shard_map/all_gather | solution.py:96
  8.3 48.7 %copy-start.4 = (f32[1,64,2048]{2,1,0:T(8,128)}, f32[1,64,2048]{2,1,0:T(8,128)S(1)}, u32[]{:S(2)}) copy-start(f32[1,64,2048]{2,1,0:T(8,128)S(1)} %convert_element_type.101) | copy-start | bytes 1572868
  20.2 0.8 copy-start.2
  23.6 33.4 %all-to-all-start.1 = ((f32[16,128,4]{1,2,0:T(4,128)}), f32[16,128,4]{1,2,0:T(4,128)S(1)}, u32[]{:S(2)}, u32[]{:S(2)}) async-start(f32[16,128,4]{1,2,0:T(4,128)} %bitcast.19), calls=%async_computation.1 | async-start | bytes 65536 | tf_op jit(solution)/shard_map/all_to_all | solution.py:97
  57.0 572.3 %all-to-all-start = ((bf16[16,3,4,32,2048]{4,3,2,1,0:T(8,128)(2,1)}), bf16[16,3,4,32,2048]{4,3,2,1,0:T(8,128)(2,1)}, u32[]{:S(2)}, u32[]{:S(2)}) async-start(bf16[16,3,4,32,2048]{4,3,2,1,0:T(8,128)(2,1)} %bitcast.117), calls=%async_computation | async-start | bytes 50331648 | tf_op jit(solution)/shard_map/all_to_all | solution.py:50
  63.0 27.0 %copy-start.10 = (s32[80]{0:T(128)S(1)}, s32[80]{0:T(128)}, u32[]{:S(2)}) copy-start(s32[80]{0:T(128)} %param.25) | copy-start | bytes 964
  692.7 781.9 %all-to-all-start.2 = ((bf16[16,5,3,32,2048]{4,3,1,2,0:T(8,128)(2,1)}), bf16[16,5,3,32,2048]{4,3,1,2,0:T(8,128)(2,1)}, u32[]{:S(2)}, u32[]{:S(2)}) async-start(bf16[16,5,3,32,2048]{4,3,1,2,0:T(8,128)(2,1)} %copy.91), calls=%async_computation.3 | async-start | bytes 62914560 | tf_op jit(solution)/shard_map/all_to_all | solution.py:122
  698.4 746.4 %copy-start.3 = (f32[64,2048]{1,0:T(8,128)S(1)}, f32[64,2048]{1,0:T(8,128)}, u32[]{:S(2)}) copy-start(f32[64,2048]{1,0:T(8,128)} %copy-done.2) | copy-start | bytes 1572868
  698.4 746.4 %copy-start.5 = (f32[1,64,2048]{2,1,0:T(8,128)S(1)}, f32[1,64,2048]{2,1,0:T(8,128)}, u32[]{:S(2)}) copy-start(f32[1,64,2048]{2,1,0:T(8,128)} %copy-done.4) | copy-start | bytes 1572868
  698.4 746.3 %reduce-scatter.2.cloned.1.call-start = ((), (), s32[]{:S(2)}) async-start(), calls=%async_computation.5 | async-start | bytes 17301504 | tf_op jit(solution)/shard_map/reduce_scatter | solution.py:109
  1444.7 51.2 %copy-start.1 = (bf16[2048,64]{0,1:T(8,128)(2,1)S(1)}, bf16[2048,64]{0,1:T(8,128)(2,1)}, u32[]{:S(2)}) copy-start(bf16[2048,64]{0,1:T(8,128)(2,1)} %param.20) | copy-start | bytes 786436
Sparse Core Ops, SparseCore 0:
  18.3 115.4 all-gather.1
  701.5 743.1 reduce-scatter.1

commit v2 on v1

--- a/solution.py
+++ b/solution.py
@@ -44,10 +44,19 @@
     old_total = old_slots.shape[0]
     column = inputs_one.shape[1]
     own_rows = column // slice_count
-    moving = jnp.transpose(
-        weights_local.reshape(index_count, piece_rows, 3, old_width, D), (0, 2, 3, 1, 4)
-    )
-    spread = lax.all_to_all(moving, "expert", split_axis=0, concat_axis=0, tiled=True)
+    parts = 2 if piece_rows % 2 == 0 else 1
+    part_rows = piece_rows // parts
+    pieces = weights_local.reshape(index_count, parts, part_rows, 3, old_width, D)
+    spreads = [
+        lax.all_to_all(
+            jnp.transpose(pieces[:, part], (0, 2, 3, 1, 4)),
+            "expert",
+            split_axis=0,
+            concat_axis=0,
+            tiled=True,
+        )
+        for part in range(parts)
+    ]
     shape = (column, HEADS, HEAD_DIM)
     scores = jnp.einsum(
         "thd,uhd->htu",
@@ -84,43 +93,58 @@
         slot_hot = (old_slots[None, :] == expert_ids[:, None]).astype(jnp.float32)
         return jnp.dot(gates, slot_hot, precision=lax.Precision.HIGHEST)
 
-    def side_by_side(one, two):
-        split = (slice_count, 1, own_rows, one.shape[-1])
-        return jnp.concatenate([one.reshape(split), two.reshape(split)], 1).reshape(
-            2 * column, one.shape[-1]
+    start = lax.axis_index("dp") * own_rows
+
+    def own_share(one, two):
+        return jnp.concatenate(
+            [lax.dynamic_slice_in_dim(part, start, own_rows, 0) for part in (one, two)], 0
         )
 
-    gates = side_by_side(
-        slot_gates(normed_one, routes_one[0]), slot_gates(normed_two, routes_two[0])
+    def gather_all(share):
+        return lax.all_gather(
+            lax.all_gather(share, "expert", tiled=True), "dp", tiled=True
+        )
+
+    tokens = gather_all(own_share(normed_one, normed_two))
+    gates = gather_all(
+        own_share(slot_gates(normed_one, routes_one[0]), slot_gates(normed_two, routes_two[0]))
     )
-    tokens = lax.all_gather(side_by_side(normed_one, normed_two), "expert", tiled=True)
-    own_gates = lax.all_to_all(
-        jnp.moveaxis(gates.reshape(2 * column, index_count, old_width), 1, 0),
-        "expert",
-        split_axis=0,
-        concat_axis=0,
-        tiled=True,
-    ).reshape(index_count * 2 * column, old_width)
-    first = jnp.einsum("td,nsfd->tnsf", tokens, moving[:, 0], preferred_element_type=jnp.float32)
-    second = jnp.einsum("td,nsfd->tnsf", tokens, moving[:, 1], preferred_element_type=jnp.float32)
-    act = (jax.nn.silu(first) * second * own_gates[:, None, :, None]).astype(jnp.bfloat16)
-    mixed = jnp.einsum("tnsf,nsfd->td", act, moving[:, 2], preferred_element_type=jnp.float32)
-    spread, mixed = lax.optimization_barrier((spread, mixed))
-    summed = lax.psum_scatter(mixed, ("expert", "dp"), scatter_dimension=0, tiled=True)
-    summed = summed.reshape(2, own_rows, D)
-    start = lax.axis_index("dp") * own_rows
-    own_one = lax.dynamic_slice_in_dim(hidden_one, start, own_rows, 0)
-    own_two = lax.dynamic_slice_in_dim(hidden_two, start, own_rows, 0)
-    output_one = (own_one + summed[0]).astype(jnp.bfloat16)[None]
-    output_two = (own_two + summed[1]).astype(jnp.bfloat16)[None]
+    own_gates = lax.dynamic_slice_in_dim(
+        gates, lax.axis_index("expert") * old_width, old_width, 1
+    )
+    first = jnp.einsum(
+        "td,fsd->tsf", tokens, weights_local[:, 0], preferred_element_type=jnp.float32
+    )
+    second = jnp.einsum(
+        "td,fsd->tsf", tokens, weights_local[:, 1], preferred_element_type=jnp.float32
+    )
+    act = (jax.nn.silu(first) * second * own_gates[:, :, None]).astype(jnp.bfloat16)
+    mixed = jnp.einsum(
+        "tsf,fsd->td", act, weights_local[:, 2], preferred_element_type=jnp.float32
+    )
+    summed = lax.psum_scatter(mixed, "dp", scatter_dimension=0, tiled=True)
+    summed = lax.psum_scatter(summed, "expert", scatter_dimension=0, tiled=True)
+    outputs = (own_share(hidden_one, hidden_two) + summed).astype(jnp.bfloat16)
+    output_one = outputs[None, :own_rows]
+    output_two = outputs[None, own_rows:]
 
-    table = jnp.moveaxis(spread, 2, 1).reshape(index_count * old_width, 3, piece_rows, D)
     new_place = jnp.sum(
         jnp.where(new_slots[:, None] == expert_ids[None, :], old_place[None, :], 0), 1
     )
-    outgoing = table[new_place].reshape(index_count, new_width, 3, piece_rows, D)
-    arrived = lax.all_to_all(outgoing, "expert", split_axis=0, concat_axis=0, tiled=True)
-    weights_new = jnp.transpose(arrived, (0, 3, 2, 1, 4)).reshape(hidden_rows, 3, new_width, D)
+    weights_new = jnp.zeros(
+        (3, new_width, index_count, parts, part_rows, D), weights_local.dtype
+    )
+    for part in range(parts):
+        table = jnp.moveaxis(spreads[part], 2, 1).reshape(
+            index_count * old_width, 3, part_rows, D
+        )
+        outgoing = table[new_place].reshape(index_count, new_width, 3, part_rows, D)
+        arrived = lax.all_to_all(outgoing, "expert", split_axis=0, concat_axis=0, tiled=True)
+        weights_new = lax.optimization_barrier(
+            weights_new.at[:, :, :, part].set(jnp.transpose(arrived, (2, 1, 0, 3, 4)))
+        )
+    weights_new = weights_new.reshape(3, new_width, hidden_rows, D)
+    weights_new = jnp.transpose(weights_new, (2, 0, 1, 3))
     return (output_one, output_two, weights_new[None])
 
 

time: 1500 us -> 1470 us (0.980)
  waiting for transfers between devices: 1240 us -> 1060 us
  blocking collectives: 0 us -> 128 us
    reduce_scatter x1 -> x2, waiting for transfers between devices: 746 us -> 0.02 us  [the longest x1 0.02 us: shards(): summed = lax.psum_scatter(mixed, 'dp', scatter_dimension=0, tiled=True)]
    all_to_all x1 -> x2, waiting for transfers between devices: 28 us -> 613 us  [shards(): lax.all_to_all(outgoing, 'expert', split_axis=0, concat_axis=0, tiled=True)]
    all_to_all x2, waiting for transfers between devices: 419 us -> 261 us  [shards(): lax.all_to_all(jnp.transpose(pieces[:, part], (0, 2, 3, 1, 4)), 'expert',...]
    all_gather x1 -> x2, waiting for transfers between devices: 43 us -> 189 us  [the longest x1 189 us: gather_all(): lax.all_gather(share, 'expert', tiled=True)]
    all_gather x0 -> x2, blocking collectives: none -> 128 us  [the longest x1 114 us: gather_all(): lax.all_gather(share, 'expert', tiled=True)]
    scatter x0 -> x2, local copies, waits for them, and re-layouts: none -> 29.6 us  [shards(): weights_new.at[:, :, :, part].set(jnp.transpose(arrived, (2, 1, 0, 3, 4)))]
    another operation x2 -> x0, local copies, waits for them, and re-layouts: 27.6 us -> none  [the longest x1 26.8 us: shards(): weights_local.reshape(index_count, piece_rows, 3, old_width, D)]
    unnamed x26 -> x39, local copies, waits for them, and re-layouts: 3.92 us -> 27.6 us
  transfers between devices with their start and end apart: 5 -> 8, of which waited for: 4 -> 4; matrix products, arithmetic and copies ran while one was open for 9% -> 13% of each run, Pallas kernels for 0% -> 0%
where the time goes in v2:
time: 1470 us
  waiting for transfers between devices  1060 us (72%)
  local copies, waits for them, and re-layouts  160 us (11%)
  blocking collectives  128 us (9%)
  matrix products  77.2 us (5%)
  starting transfers between devices  22.8 us (2%)
    all_to_all x2, waiting for transfers between devices, shards(): lax.all_to_all(outgoing, 'expert', split_axis=0, concat_axis=0, tiled=True)  613 us
    all_to_all x2, waiting for transfers between devices, shards(): lax.all_to_all(jnp.transpose(pieces[:, part], (0, 2, 3, 1, 4)), 'expert',...  261 us
    all_gather x1, waiting for transfers between devices, gather_all(): lax.all_gather(share, 'expert', tiled=True)  189 us
    all_gather x1, blocking collectives, gather_all(): lax.all_gather(share, 'expert', tiled=True)  114 us
    transpose x3, local copies, waits for them, and re-layouts, shards(): jnp.transpose(pieces[:, part], (0, 2, 3, 1, 4))  32.4 us
    scatter x2, local copies, waits for them, and re-layouts, shards(): weights_new.at[:, :, :, part].set(jnp.transpose(arrived, (2, 1, 0, 3, 4)))  29.6 us
  transfers between devices with their start and end apart: 8, of which 4 were waited for; matrix products, arithmetic and copies ran while one was open for 13% of the time, Pallas kernels for 0%

profile of v2, /device:TPU:15, one launch (start us, length us, event | category | flops | bytes accessed | tf_op | source)
XLA Modules:
  0.0 1470.9 jit_solution(11331297457369516331)
XLA Ops:
  7.2 21.8 %copy.99 = bf16[1,512,3,4,2048]{4,1,3,2,0:T(8,128)(2,1)S(1)} copy(bf16[1,512,3,4,2048]{4,3,2,1,0:T(4,128)(2,1)} %param.25) | data formatting | bytes 50331648 | tf_op args[8]
  29.0 11.0 slice_bitcast_fusion
  40.0 5.5 copy-done.2
  45.5 10.7 copy.75
  56.2 6.6 all-to-all-start
  62.8 10.7 copy.77
  73.5 261.4 %all-to-all-done = bf16[16,3,4,16,2048]{4,3,2,1,0:T(8,128)(2,1)} async-done(((bf16[16,3,4,16,2048]{4,3,2,1,0:T(8,128)(2,1)}), bf16[16,3,4,16,2048]{4,3,2,1,0:T(8,128)(2,1)}, u32[]{:S(2)}, u32[]{:S(2)}) %all-to-all-start) | async-done | bytes 12582944 | tf_op jit(solution)/shard_map/all_to_all | solution.py:51
  335.0 4.9 all-to-all-start.2
  340.2 0.1 copy.85
  340.3 0.2 fusion.23
  340.5 0.3 fusion.12
  340.8 0.1 fusion.47
  341.0 0.5 fusion.27
  341.5 1.0 multiply_convert_fusion
  342.5 0.7 pad_maximum_fusion
  343.3 189.0 %all-gather.3.cloned.1.call-done = bf16[1024,2048]{1,0:T(8,128)(2,1)} async-done(((bf16[64,2048]{1,0:T(8,128)(2,1)}), bf16[1024,2048]{1,0:T(8,128)(2,1)}) %all-gather.3.cloned.1.call-update) | async-done | bytes 4194320 | tf_op jit(solution)/shard_map/all_gather | solution.py:105
  532.4 0.2 fusion.33
  532.6 0.1 copy.70
  532.8 0.2 fusion.34
  532.9 0.1 copy.72
  533.0 0.2 fusion.49
  533.3 0.2 fusion.37
  533.5 0.2 fusion.48
  533.8 0.2 fusion.35
  534.0 114.4 %all_gather.14 = f32[1024,64]{1,0:T(8,128)S(1)} all-gather(f32[64,64]{1,0:T(8,128)S(1)} %pad_maximum_fusion.1), channel_id=1, replica_groups=mesh['dp'=2,'expert'=16] {'expert'}, dimensions={0}, use_global_device_ids=true | all-gather | bytes 278528 | tf_op jit(solution)/shard_map/all_gather | solution.py:105
  648.5 14.0 all_gather.15
  662.5 0.3 constant_dynamic-slice_fusion
  662.8 0.3 copy.73
  663.2 0.1 select_reduce_fusion.1
  663.3 0.1 select_reduce_fusion
  663.4 10.7 copy.76
  674.1 12.8 gather_fusion
  686.9 5.9 all-to-all-start.1
  692.8 0.2 reduce-scatter.3.cloned.1.call-start
  693.0 24.4 %fusion.7 = f32[2048,512,4]{1,0,2:T(8,128)} fusion(bf16[512,3,4,2048]{3,0,2,1:T(8,128)(2,1)} %bitcast.128, bf16[2048,2048]{1,0:T(8,128)(2,1)} %all-gather.5.cloned.1.call-done), kind=kOutput, calls=%fused_computation.19 | convolution fusion | flops 17179869184 | bytes 33554432 | tf_op jit(solution)/shard_map/td,fsd->tsf/dot_general | solution.py:115
  717.4 27.0 %fusion.2 = bf16[2048,4,512]{2,0,1:T(8,128)(2,1)} fusion(f32[2048,512,4]{1,0,2:T(8,128)} %fusion.7, bf16[512,3,4,2048]{3,0,2,1:T(8,128)(2,1)} %bitcast.129, bf16[2048,2048]{1,0:T(8,128)(2,1)} %all-gather.5.cloned.1.call-done, f32[2048,4]{0,1:T(4,128)S(1)} %copy.73), kind=kOutput, calls=%fused_computation.5 | convolution fusion | flops 17209229312 | bytes 41975808 | tf_op jit(solution)/shard_map/td,fsd->tsf/dot_general | solution.py:118
  744.4 24.1 %convolution_bitcast_fusion = f32[2048,2048]{1,0:T(8,128)} fusion(bf16[2048,4,512]{2,0,1:T(8,128)(2,1)} %fusion.2, bf16[512,3,4,2048]{3,0,2,1:T(8,128)(2,1)} %bitcast.130), kind=kOutput, calls=%fused_computation.14 | convolution fusion | flops 17179869184 | bytes 33554432 | tf_op jit(solution)/shard_map/tsf,fsd->td/dot_general | solution.py:122
  768.5 10.9 copy.78
  779.4 13.3 gather_fusion.1
  792.7 239.7 %all-to-all-done.1 = bf16[16,5,3,16,2048]{4,3,2,1,0:T(8,128)(2,1)} async-done(((bf16[16,5,3,16,2048]{4,3,2,1,0:T(8,128)(2,1)}), bf16[16,5,3,16,2048]{4,3,2,1,0:T(8,128)(2,1)}, u32[]{:S(2)}, u32[]{:S(2)}) %all-to-all-start.1) | async-done | bytes 15728672 | tf_op jit(solution)/shard_map/all_to_all | solution.py:142
  1032.4 5.1 all-to-all-start.3
  1037.6 0.5 reduce-scatter.5.cloned.1.call-update
  1038.3 16.0 %scatter.6 = bf16[3,5,16,2,16,2048]{5,4,0,1,2,3:T(8,128)(2,1)} pad(bf16[3,5,16,1,16,2048]{5,4,0,1,2,3:T(8,128)(2,1)} %bitcast.26, bf16[]{:T(256)} %constant.93.clone.1), padding=0_0x0_0x0_0x0_1x0_0x0_0 | pad | bytes 47185920 | tf_op jit(solution)/shard_map/scatter | solution.py:144
  1054.3 373.3 %all-to-all-done.3 = bf16[16,5,3,16,2048]{4,3,2,1,0:T(8,128)(2,1)} async-done(((bf16[16,5,3,16,2048]{4,3,2,1,0:T(8,128)(2,1)}), bf16[16,5,3,16,2048]{4,3,2,1,0:T(8,128)(2,1)}, u32[]{:S(2)}, u32[]{:S(2)}) %all-to-all-start.3) | async-done | bytes 15728672 | tf_op jit(solution)/shard_map/all_to_all | solution.py:142
  1427.6 13.6 bitcast_dynamic-update-slice_fusion
  1441.2 21.4 %copy.79 = bf16[3,5,16,2,16,2048]{5,4,3,2,1,0:T(8,128)(2,1)} copy(bf16[3,5,16,2,16,2048]{5,4,0,1,2,3:T(8,128)(2,1)} %bitcast_dynamic-update-slice_fusion) | data formatting | bytes 62914560 | tf_op jit(solution)/shard_map/optimization_barrier | solution.py:143
  1462.6 1.1 fusion.22
  1463.7 0.7 slice_bitcast_fusion.10
  (60 shorter events, 0.9 us)
Async XLA Ops:
  7.2 525.9 %copy-start = (bf16[2048,64]{0,1:T(8,128)(2,1)S(1)}, bf16[2048,64]{0,1:T(8,128)(2,1)}, u32[]{:S(2)}) copy-start(bf16[2048,64]{0,1:T(8,128)(2,1)} %param.24) | copy-start | bytes 786436
  29.0 16.5 %copy-start.2 = (bf16[1,512,3,4,2048]{4,1,3,2,0:T(8,128)(2,1)}, bf16[1,512,3,4,2048]{4,1,3,2,0:T(8,128)(2,1)S(1)}, u32[]{:S(2)}) copy-start(bf16[1,512,3,4,2048]{4,1,3,2,0:T(8,128)(2,1)S(1)} %copy.99) | copy-start | bytes 75497472
  56.2 278.8 %all-to-all-start = ((bf16[16,3,4,16,2048]{4,3,2,1,0:T(8,128)(2,1)}), bf16[16,3,4,16,2048]{4,3,2,1,0:T(8,128)(2,1)}, u32[]{:S(2)}, u32[]{:S(2)}) async-start(bf16[16,3,4,16,2048]{4,3,2,1,0:T(8,128)(2,1)} %copy.75), calls=%async_computation.2 | async-start | bytes 25165824 | tf_op jit(solution)/shard_map/all_to_all | solution.py:51
  73.5 266.5 %copy-start.7 = (bf16[1,64,2048]{2,1,0:T(8,128)(2,1)S(1)}, bf16[1,64,2048]{2,1,0:T(8,128)(2,1)}, u32[]{:S(2)}) copy-start(bf16[1,64,2048]{2,1,0:T(8,128)(2,1)} %param.18) | copy-start | bytes 786436
  73.5 266.6 %copy-start.8 = (bf16[1,64,2048]{2,1,0:T(8,128)(2,1)S(1)}, bf16[1,64,2048]{2,1,0:T(8,128)(2,1)}, u32[]{:S(2)}) copy-start(bf16[1,64,2048]{2,1,0:T(8,128)(2,1)} %param.19) | copy-start | bytes 786436
  73.5 266.6 %copy-start.9 = (bf16[1,64,2048]{2,1,0:T(8,128)(2,1)S(1)}, bf16[1,64,2048]{2,1,0:T(8,128)(2,1)}, u32[]{:S(2)}) copy-start(bf16[1,64,2048]{2,1,0:T(8,128)(2,1)} %param.20) | copy-start | bytes 786436
  73.5 266.7 %copy-start.6 = (bf16[1,64,2048]{2,1,0:T(8,128)(2,1)S(1)}, bf16[1,64,2048]{2,1,0:T(8,128)(2,1)}, u32[]{:S(2)}) copy-start(bf16[1,64,2048]{2,1,0:T(8,128)(2,1)} %param.17) | copy-start | bytes 786436
  73.5 266.8 %copy-start.3 = (bf16[1,64,2048]{2,1,0:T(8,128)(2,1)S(1)}, bf16[1,64,2048]{2,1,0:T(8,128)(2,1)}, u32[]{:S(2)}) copy-start(bf16[1,64,2048]{2,1,0:T(8,128)(2,1)} %param.22) | copy-start | bytes 786436
  73.5 267.0 %copy-start.14 = (s32[1,64]{1,0:T(1,128)S(1)}, s32[1,64]{1,0:T(1,128)}, u32[]{:S(2)}) copy-start(s32[1,64]{1,0:T(1,128)} %param.21) | copy-start | bytes 772
  73.5 268.0 %copy-start.10 = (f32[2048]{0:T(1024)S(1)}, f32[2048]{0:T(1024)}, u32[]{:S(2)}) copy-start(f32[2048]{0:T(1024)} %param.23) | copy-start | bytes 24580
  73.5 458.8 %copy-start.12 = (s32[1,64,8]{1,2,0:T(8,128)S(1)}, s32[1,64,8]{1,2,0:T(8,128)}, u32[]{:S(2)}) copy-start(s32[1,64,8]{1,2,0:T(8,128)} %param.26) | copy-start | bytes 6148
  73.5 459.1 %copy-start.13 = (s32[1,64,8]{1,2,0:T(8,128)S(1)}, s32[1,64,8]{1,2,0:T(8,128)}, u32[]{:S(2)}) copy-start(s32[1,64,8]{1,2,0:T(8,128)} %param.27) | copy-start | bytes 6148
  73.5 459.8 %copy-start.15 = (s32[64]{0:T(128)S(1)}, s32[64]{0:T(128)}, u32[]{:S(2)}) copy-start(s32[64]{0:T(128)} %param.28) | copy-start | bytes 772
  335.0 351.9 %all-to-all-start.2 = ((bf16[16,3,4,16,2048]{4,3,2,1,0:T(8,128)(2,1)}), bf16[16,3,4,16,2048]{4,3,2,1,0:T(8,128)(2,1)}, u32[]{:S(2)}, u32[]{:S(2)}) async-start(bf16[16,3,4,16,2048]{4,3,2,1,0:T(8,128)(2,1)} %copy.77), calls=%async_computation.4 | async-start | bytes 25165824 | tf_op jit(solution)/shard_map/all_to_all | solution.py:51
  339.9 323.4 %copy-start.16 = (s32[80]{0:T(128)S(1)}, s32[80]{0:T(128)}, u32[]{:S(2)}) copy-start(s32[80]{0:T(128)} %param.29) | copy-start | bytes 964
  339.9 192.4 %all-gather.3.cloned.1.call-start = ((), (), s32[]{:S(2)}) async-start(), calls=%async_computation.6 | async-start | bytes 4456448 | tf_op jit(solution)/shard_map/all_gather | solution.py:105
  343.2 349.8 %all-gather.5.cloned.1.call-start = ((), (), s32[]{:S(2)}) async-start(), calls=%async_computation.7 | async-start | bytes 12582912 | tf_op jit(solution)/shard_map/all_gather | solution.py:104
  663.4 23.5 %copy-start.11 = (s32[1024]{0:T(1024)}, s32[1024]{0:T(1024)S(1)}, u32[]{:S(2)}) copy-start(s32[1024]{0:T(1024)S(1)} %pad_clamp_fusion) | copy-start | bytes 12292
  686.9 345.5 %all-to-all-start.1 = ((bf16[16,5,3,16,2048]{4,3,2,1,0:T(8,128)(2,1)}), bf16[16,5,3,16,2048]{4,3,2,1,0:T(8,128)(2,1)}, u32[]{:S(2)}, u32[]{:S(2)}) async-start(bf16[16,5,3,16,2048]{4,3,2,1,0:T(8,128)(2,1)} %bitcast.133), calls=%async_computation.3 | async-start | bytes 31457280 | tf_op jit(solution)/shard_map/all_to_all | solution.py:142
  692.8 344.9 %reduce-scatter.3.cloned.1.call-start = ((), (), s32[]{:S(2)}) async-start(), calls=%async_computation.8 | async-start | bytes 25165824 | tf_op jit(solution)/shard_map/reduce_scatter | solution.py:125
  1032.4 5.7 copy-start.4
  1032.4 5.8 copy-start.5
  1032.4 395.2 %all-to-all-start.3 = ((bf16[16,5,3,16,2048]{4,3,2,1,0:T(8,128)(2,1)}), bf16[16,5,3,16,2048]{4,3,2,1,0:T(8,128)(2,1)}, u32[]{:S(2)}, u32[]{:S(2)}) async-start(bf16[16,5,3,16,2048]{4,3,2,1,0:T(8,128)(2,1)} %bitcast.134), calls=%async_computation.5 | async-start | bytes 31457280 | tf_op jit(solution)/shard_map/all_to_all | solution.py:142
  1037.6 425.0 %reduce-scatter.5.cloned.1.call-start = ((), (), s32[]{:S(2)}) async-start(), calls=%async_computation.9 | async-start | bytes 8912896 | tf_op jit(solution)/shard_map/reduce_scatter | solution.py:126
  1441.2 23.2 %copy-start.1 = (bf16[2048,64]{0,1:T(8,128)(2,1)S(1)}, bf16[2048,64]{0,1:T(8,128)(2,1)}, u32[]{:S(2)}) copy-start(bf16[2048,64]{0,1:T(8,128)(2,1)} %param.24) | copy-start | bytes 786436
Sparse Core Ops, SparseCore 0:
  343.4 188.8 all-gather.2
  533.8 108.7 all-gather.4
  768.7 188.7 reduce-scatter.2
  1042.7 291.0 reduce-scatter.4
